TPU v7x, 32 devices: a whole 2x2x4 slice. The times are simulated.
32 devices in a mesh: dp: 8 (over z, x), mp: 4 (over y, core).
Axes of the slice: x: 2, y: 2, z: 4, core: 2. Of those that a mesh axis runs over, the one named last changes fastest.
Arguments:
- patches: bfloat16 [128, 196, 384], P(('dp', 'mp')), may hold values from -6 to 6
- qkv_weight: bfloat16 [2, 384, 1152], P(None, None, 'mp'), may hold values from -0.3125 to 0.3125
- proj_weight: bfloat16 [2, 384, 384], P(None, None, 'mp'), may hold values from -0.875 to 0.875
- core_up: bfloat16 [2, 384, 1536], P(None, None, 'mp'), may hold values from -0.3125 to 0.3125
- core_down: bfloat16 [2, 1536, 384], P(None, None, 'mp'), may hold values from -1.25 to 1.25
- residual_up: bfloat16 [2, 8, 384, 1536], P(None, 'dp'), may hold values from -0.15625 to 0.15625
- residual_down: bfloat16 [2, 8, 1536, 384], P(None, 'dp'), may hold values from -0.625 to 0.625
- position_bias: float32 [2, 169, 12], replicated, may hold values from -6 to 6
- router_weight: bfloat16 [2, 384, 8], replicated, may hold values from -0.21875 to 0.21875
- norm_gain: float32 [2, 2, 384], replicated, may hold values from 0.5 to 1.5
- norm_bias: float32 [2, 2, 384], replicated, may hold values from -1.25 to 1.25
- cotangent: bfloat16 [128, 196, 384], P(('dp', 'mp')), may hold values from -6 to 6
- image_valid: int32 [128], P(('dp', 'mp')), may hold values from 0 to 1, as said below
- expert_index: int32 [128, 196], P(('dp', 'mp')), may hold values from 0 to 7
- slot_index: int32 [128, 196], P(('dp', 'mp')), may hold values from -1 to 121, as said below
- region_id: int32 [128, 14, 14], P(('dp', 'mp')), may hold values from 0 to 3
Outputs:
- block_output: bfloat16 [128, 196, 384], P(('dp', 'mp'))
- input_grad: float32 [128, 196, 384], P(('dp', 'mp'))
- qkv_grad: float32 [2, 384, 1152], P(None, None, 'mp')
- proj_grad: float32 [2, 384, 384], P(None, None, 'mp')
- core_up_grad: float32 [2, 384, 1536], P(None, None, 'mp')
- core_down_grad: float32 [2, 1536, 384], P(None, None, 'mp')
- residual_up_grad: float32 [2, 8, 384, 1536], P(None, 'dp')
- residual_down_grad: float32 [2, 8, 1536, 384], P(None, 'dp')
- position_grad: float32 [2, 169, 12], replicated
- router_grad: float32 [2, 384, 8], replicated
- gain_grad: float32 [2, 2, 384], replicated
- bias_grad: float32 [2, 2, 384], replicated
Inputs may be any that keep to these rules, and one draw needn't show every extreme that they name: `image_valid`: on each device (the 4 image slots of one index of dp+mp) the real images come first, and there are 4 or 2 of them. `slot_index`: among the tokens of one device, each pair of expert and slot belongs to at most one token; tokens of padding slots have -1.
All inputs are finite; a program needn't handle non-finite values.
Results may differ from a plain program's by a relative error of at most 0.024.
Values may be sent and summed in bfloat16 or wider, within the bound.
A program may use at most 192 MiB of HBM per device.

v0:
```python
import functools

import jax
import jax.numpy as jnp
import numpy as np
from jax import lax
from jax.experimental import pallas as pl
from jax.experimental.pallas import tpu as pltpu
from jax.sharding import PartitionSpec as P

HEADS = 12
HEAD_DIM = 32
EXPERTS = 8
WINDOW = 7
GRID = 14
SHIFT = 3
LAYERS = 2
WINPOS = 49
OFFSETS = 169
CAP = 122

WPAD = 64
IMGROWS = 256
PATCHES = 196
SLOTS = 128
ROWS = EXPERTS * SLOTS
LANES = 128
GROUP = 4
PAIRS = 2
TABLE = 256

bf16 = jnp.bfloat16
f32 = jnp.float32
highest = lax.Precision.HIGHEST
norm_epsilon = 1e-05
mask_fill = -100.0
head_scale = HEAD_DIM ** (-0.5)
MESH = pl.DeviceIdType.MESH
MIB = 1024 * 1024


def nn(a, b):
    return lax.dot_general(a, b, (((1,), (0,)), ((), ())), preferred_element_type=f32)


def nt(a, b):
    return lax.dot_general(a, b, (((1,), (1,)), ((), ())), preferred_element_type=f32)


def tn(a, b):
    return lax.dot_general(a, b, (((0,), (0,)), ((), ())), preferred_element_type=f32)


def iota(shape, dim):
    return lax.broadcasted_iota(jnp.int32, shape, dim)


def onehot(flags):
    return jnp.where(flags, 1.0, 0.0).astype(bf16)


def natural_of_row(shifted):
    moved = SHIFT if shifted else 0
    blocks = GRID // WINDOW
    out = -np.ones(IMGROWS, np.int32)
    for window in range(blocks * blocks):
        for cell in range(WINPOS):
            row = (window // blocks * WINDOW + cell // WINDOW + moved) % GRID
            col = (window % blocks * WINDOW + cell % WINDOW + moved) % GRID
            out[window * WPAD + cell] = row * GRID + col
    return out


def key_base_of(key):
    return (2 * WINDOW) * (WINDOW - 1) - (key // WINDOW * (2 * WINDOW - 1) + key % WINDOW)


def enter_table():
    held = natural_of_row(False)
    return (held[:, None] == np.arange(PATCHES)[None, :]).astype(np.float32)


def move_table(shifted):
    first, second = natural_of_row(False), natural_of_row(shifted)
    same = (second[:, None] == first[None, :]) & (second[:, None] >= 0)
    return same.astype(np.float32)


def cell_entries():
    cell = np.arange(LANES) % WPAD
    return np.where(cell < WINPOS, cell // WINDOW * (2 * WINDOW - 1) + cell % WINDOW, -4 * TABLE).astype(np.int32)


def norm_parts(x):
    width = x.shape[-1]
    center = x - jnp.sum(x, -1, keepdims=True) * (1.0 / width)
    spread = jnp.sum(center * center, -1, keepdims=True) * (1.0 / width)
    rstd = lax.rsqrt(spread + norm_epsilon)
    return center * rstd, rstd


def norm_back(grad, gain, xhat, rstd):
    width = xhat.shape[-1]
    dxhat = grad * gain
    mean_one = jnp.sum(dxhat, -1, keepdims=True) * (1.0 / width)
    mean_two = jnp.sum(dxhat * xhat, -1, keepdims=True) * (1.0 / width)
    return rstd * (dxhat - mean_one - xhat * mean_two)


def split_two(x):
    high = x.astype(bf16)
    return high, (x - high.astype(f32)).astype(bf16)


def collect(pos_col, returned_ref):
    pick = onehot(pos_col == iota((pos_col.shape[0], ROWS), 1))
    out = nn(pick, returned_ref[0])
    for piece in range(1, returned_ref.shape[0]):
        out = out + nn(pick, returned_ref[piece])
    return out


def join(ref):
    return ref[...].reshape(ref.shape[0] * ref.shape[1], *ref.shape[2:])


def store(ref, rows):
    ref[...] = rows.reshape(ref.shape).astype(ref.dtype)


def per_image(function, count):
    return jnp.concatenate([function(i) for i in range(count)], 0)


def image_rows(i):
    return slice(i * IMGROWS, (i + 1) * IMGROWS)


def lay_positions(row_ref):
    return jnp.concatenate([row_ref[i, 0:1, :] for i in range(row_ref.shape[0])], 1)


def spread_rows(pos_row, rows_low):
    return nn(onehot(iota((ROWS, pos_row.shape[1]), 0) == pos_row), rows_low)


def route(second_low, router, pos_col):
    logits = nt(second_low, router)
    lane = iota(logits.shape, 1)
    logits = jnp.where(lane < EXPERTS, logits, -1e30)
    expo = jnp.exp(logits - jnp.max(logits, -1, keepdims=True))
    probs = expo / jnp.sum(expo, -1, keepdims=True)
    expert = jnp.where(pos_col >= 0, pos_col // SLOTS, -1)
    chosen = jnp.where(lane == expert, 1.0, 0.0)
    return probs, chosen, jnp.sum(probs * chosen, -1, keepdims=True)


def head_masks():
    rows = iota((LANES, LANES), 0) // HEAD_DIM
    return [onehot(rows == h) for h in range(GROUP)]


def lane_masks():
    lane = iota((WPAD, LANES), 1)
    return [onehot(lane < WPAD), onehot(lane >= WPAD)]


def keys_entry(cells, key_row, turned):
    parts = [cells + (key_base_of(col) - key_row * (2 * WINDOW - 1)) for col in range(WINDOW)]
    return jnp.concatenate(parts, 0 if turned else 1)


def form_bias(bias_ref, table_ref, entry_row):
    layers, heads = bias_ref.shape[:2]
    lines = layers * heads
    bias_ref[...] = jnp.where(iota(bias_ref.shape, 2) < WINPOS, 0.0, -1e30)
    table = table_ref[...]
    high = table.astype(bf16)
    mid, low = split_two(table - high.astype(f32))
    parts = jnp.concatenate([high.astype(f32), mid.astype(f32), low.astype(f32)], 0).astype(bf16)

    def step(key_row, carry):
        pick = onehot(iota((TABLE, WINDOW * LANES), 0) == keys_entry(entry_row, key_row, False))
        rows = nn(parts, pick)
        rows = rows[:lines] + rows[lines : 2 * lines] + rows[2 * lines :]
        for col in range(WINDOW):
            for layer in range(layers):
                part = rows[layer * heads : (layer + 1) * heads, col * LANES : (col + 1) * LANES]
                bias_ref[layer, :, pl.ds(key_row * WINDOW + col, 1), :] = part.reshape(heads, 1, LANES)
        return carry

    lax.fori_loop(0, WINDOW, step, 0)


def table_grad(parts, entry_col):
    heads = parts[0].shape[0]
    lines = heads * len(parts)

    def step(key_row, total):
        keys = [
            jnp.concatenate([ref[:, pl.ds(key_row * WINDOW + col, 1), :].reshape(heads, LANES) for ref in parts], 0)
            for col in range(WINDOW)
        ]
        rows = jnp.concatenate(keys, 1)
        high = rows.astype(bf16).astype(f32)
        both = jnp.concatenate([high, rows - high], 0).astype(bf16)
        entry = keys_entry(entry_col, key_row, True)
        out = nn(both, onehot(iota((WINDOW * LANES, TABLE), 1) == entry))
        return total + out[:lines] + out[lines:]

    return lax.fori_loop(0, WINDOW, step, jnp.zeros((lines, TABLE), f32))


def attention_forward_kernel(first, shifted, mp, gather, *refs):
    refs = list(refs)
    if first:
        patches_ref, enter_ref = refs[:2]
        refs = refs[2:]
    else:
        prev_ref, prev_gate_ref, returned_ref = refs[:3]
        refs = refs[3:]
    (
        valid_ref, col_ref, row_ref, qkv_ref, proj_ref, bias_ref, move_ref, back_ref, gain_ref, nbias_ref, router_ref,
    ) = refs[:11]
    gain_ref, nbias_ref, router_ref = (ref.at[0] for ref in (gain_ref, nbias_ref, router_ref))
    refs = refs[11:]
    if first:
        table_ref, entry_ref = bias_ref, refs.pop(0)
    if gather:
        core_up_ref, core_down_ref = refs[:2]
        refs = refs[2:]
    carried_ref = refs.pop(0)
    if first:
        biases_ref = refs.pop(0)
        bias_ref = biases_ref.at[0]
    else:
        expert_out_ref = refs.pop(0)
        bias_ref = bias_ref.at[0]
    middle_ref, second_ref, gate_ref, buffer_ref, window_ref, qk_ref, v_ref, probs_ref, att_ref, proj_full = refs[:10]
    refs = refs[10:]
    if gather:
        qkv_full = refs.pop(0)
        up_out, down_out = refs[:2]
        refs = refs[2:]
    total_ref = refs.pop(0)
    step = pl.program_id(0)
    final = pl.num_programs(0) - 1
    count, _, width = carried_ref.shape
    if gather:
        shards = [ref.at[0] for ref in (qkv_ref, proj_ref, core_up_ref, core_down_ref)]
        qkv_ref, proj_ref = refs[:2]
        moving = WeightGather(shards, [qkv_ref, proj_ref, up_out, down_out], refs[2:])

        @pl.when(step == 0)
        def _():
            pl.semaphore_wait(moving.row.greet(), 2)
            for k in (0, 1):
                moving.start(k)
            form_bias(biases_ref, table_ref, entry_ref[...])

    pos_col = join(col_ref)[:, 0:1]
    if first:
        x = per_image(lambda i: nn(enter_ref[...], patches_ref[i]), count)
    else:
        expert_out = collect(pos_col, returned_ref)
        store(expert_out_ref, expert_out)
        x = join(prev_ref) + join(prev_gate_ref) * expert_out
    store(carried_ref, x)
    xhat, _ = norm_parts(x)
    normed = (xhat * gain_ref[0:1, :] + nbias_ref[0:1, :]).astype(bf16)
    window_in = per_image(lambda i: nn(move_ref[...], normed[image_rows(i)]), count).astype(bf16)
    store(window_ref, window_in)

    @pl.when(step == 0)
    def _():
        if gather:
            for k in (0, 1):
                moving.forward(k)
            for k in (2, 3):
                moving.start(k)
            for k in (0, 1):
                moving.arrive(k)
            qkv_full[...] = join(qkv_ref)
        elif first:
            form_bias(biases_ref, table_ref, entry_ref[...])
        proj_full[...] = join(proj_ref).astype(f32).T.astype(bf16)
        total_ref[...] = jnp.zeros(total_ref.shape, f32)

    qkv = join(qkv_ref)
    turned = nt(qkv, window_in).astype(bf16)
    straight = nt(window_in, qkv[width:]).astype(bf16)
    for i in range(count):
        qk_ref[i] = turned[: 2 * width, image_rows(i)]
    store(v_ref, straight[:, width:])
    heads_rows = head_masks()
    halves = lane_masks()
    low_lane = iota((WPAD, LANES), 1) < WPAD
    if shifted:
        row_labels = [nt(row_ref[i].astype(f32).astype(bf16), move_ref[...]) for i in range(count)]
        col_labels = [nn(move_ref[...], col_ref[i].astype(f32).astype(bf16)) for i in range(count)]
    for pair in range(PAIRS * count):
        image, side = pair // PAIRS, pair % PAIRS
        across = slice(pair * LANES, (pair + 1) * LANES)
        within = slice(side * LANES, (side + 1) * LANES)
        if shifted:
            ahead = col_labels[image][side * LANES : side * LANES + WPAD, 1:2]
            behind = col_labels[image][side * LANES + WPAD : (side + 1) * LANES, 1:2]
            key_label = jnp.where(low_lane, ahead, behind)
            mask = jnp.where(key_label == row_labels[image][1:2, within], 0.0, mask_fill)
        for group in range(HEADS // GROUP):
            features = slice(group * LANES, (group + 1) * LANES)
            queries = turned[features, across]
            spread = jnp.concatenate([queries * heads_rows[h] for h in range(GROUP)], 1)
            raw = nn(straight[across, features], spread)
            for h in range(GROUP):
                head = group * GROUP + h
                part = raw[:, h * LANES : (h + 1) * LANES]
                scores = jnp.where(low_lane, part[:WPAD], part[WPAD:]) * head_scale + bias_ref[head]
                if shifted:
                    scores = scores + mask
                expo = jnp.exp(scores - jnp.max(scores, 0, keepdims=True))
                probs = (expo * (1.0 / jnp.sum(expo, 0, keepdims=True))).astype(bf16)
                probs_ref[image, side * HEADS + head] = probs
                both = jnp.concatenate([probs * halves[0], probs * halves[1]], 0)
                at = slice(head * HEAD_DIM, (head + 1) * HEAD_DIM)
                values = turned[2 * width + head * HEAD_DIM : 2 * width + (head + 1) * HEAD_DIM, across]
                att_ref[image, at, within] = nn(values, both).astype(bf16)
    attended = per_image(lambda i: nt(back_ref[...], att_ref[i]), count).astype(bf16)
    branch = nt(attended, join(proj_ref))
    middle = x + per_image(lambda i: valid_ref[step * count + i].astype(f32) * branch[image_rows(i)], count)
    store(middle_ref, middle)
    xhat, _ = norm_parts(middle)
    second_low = (xhat * gain_ref[1:2, :] + nbias_ref[1:2, :]).astype(bf16)
    store(second_ref, second_low)
    _, _, gate = route(second_low, router_ref[...], pos_col)
    store(gate_ref, gate)
    total_ref[...] += spread_rows(lay_positions(row_ref), second_low)

    @pl.when(step == final)
    def _():
        buffer_ref[...] = total_ref[...].astype(bf16)
        if gather:
            for k in (2, 3):
                moving.forward(k)
            for k in (2, 3):
                moving.arrive(k)
            for k in range(4):
                moving.sent(k)


def image_spec(array_shape, count):
    rest = tuple(array_shape[1:])
    zeros = (0,) * len(rest)
    return pl.BlockSpec((count,) + rest, lambda i: (i,) + zeros)


def whole_spec(array_shape):
    zeros = (0,) * len(array_shape)
    return pl.BlockSpec(tuple(array_shape), lambda i: zeros)


def image_call(kernel, images, arrays, outs, scratch, name, collective_id=None):
    count = 2 - images % 2

    def spec(kind, shape):
        if isinstance(kind, int):
            rest = tuple(shape[1:])
            return pl.BlockSpec((1,) + rest, lambda i: (kind,) + (0,) * len(rest))
        if kind in ("smem", "any"):
            return pl.BlockSpec(memory_space=pltpu.SMEM if kind == "smem" else pl.ANY)
        return image_spec(shape, count) if kind == "image" else whole_spec(shape)

    return pl.pallas_call(
        kernel,
        grid=(images // count,),
        out_shape=[jax.ShapeDtypeStruct(shape, dtype) for _, shape, dtype in outs],
        in_specs=[spec(kind, array.shape) for kind, array in arrays],
        out_specs=[spec(kind, shape) for kind, shape, _ in outs],
        scratch_shapes=scratch,
        compiler_params=pltpu.CompilerParams(
            vmem_limit_bytes=56 * MIB,
            dimension_semantics=("arbitrary",),
            collective_id=collective_id,
            has_side_effects=collective_id is not None,
        ),
        name=name,
    )(*[array for _, array in arrays])


def send_part(g, expert_out, second_low, router, pos_col, pos_row, logit_ref, router_grad_ref, total_ref):
    probs, chosen, gate = route(second_low, router, pos_col)
    gate_grad = jnp.where(pos_col >= 0, jnp.sum(g * expert_out, -1, keepdims=True), 0.0)
    sent = (gate * g).astype(bf16)
    logit_grad = gate_grad * gate * (chosen - probs)
    store(logit_ref, logit_grad)
    high, low = split_two(logit_grad)
    router_grad_ref[...] += tn(high, second_low) + tn(low, second_low)
    total_ref[...] += spread_rows(pos_row, sent)


def turn_kernel(
    prev_ref, gate_ref, returned_ref, cotangent_ref, enter_ref, leave_ref, col_ref, row_ref, second_ref, router_ref,
    block_ref, grad_ref, logit_ref, router_grad_ref, buffer_ref, total_ref,
):
    step = pl.program_id(0)
    count = cotangent_ref.shape[0]

    @pl.when(step == 0)
    def _():
        total_ref[...] = jnp.zeros(total_ref.shape, f32)
        router_grad_ref[...] = jnp.zeros(router_grad_ref.shape, f32)

    pos_col = join(col_ref)[:, 0:1]
    expert_out = collect(pos_col, returned_ref)
    x = (join(prev_ref) + join(gate_ref) * expert_out).astype(bf16)
    for i in range(count):
        block_ref[i] = nn(leave_ref[...], x[image_rows(i)]).astype(bf16)
    g = per_image(lambda i: nn(enter_ref[...], cotangent_ref[i]), count)
    store(grad_ref, g)
    send_part(
        g, expert_out, join(second_ref), router_ref[0], pos_col, lay_positions(row_ref), logit_ref, router_grad_ref, total_ref
    )

    @pl.when(step == pl.num_programs(0) - 1)
    def _():
        buffer_ref[...] = total_ref[...].astype(bf16)


def attention_backward_kernel(last, dp, mp, fast, *refs):
    (
        valid_ref, grad_ref, returned_ref, logit_ref, middle_ref, carried_ref, router_ref, col_ref, move_ref, back_ref,
        gain_ref, proj_ref, qkv_ref, window_ref, qk_ref, v_ref, probs_ref, att_ref,
    ) = refs[:18]
    refs = refs[18:]
    refs = list(refs)
    if fast:
        units_ref = refs.pop(0)
    if last:
        leave_ref = refs.pop(0)
        if fast:
            table_above, small_above, router_above, router_here, entry_ref, half_above, down_above, attn_above = refs[:8]
            refs = refs[8:]
    else:
        row_ref, expert_out_ref, second_ref, router_next_ref = refs[:4]
        refs = refs[4:]
    out_ref = refs.pop(0)
    closing = None
    if fast and last:
        results, refs = refs[:4], refs[4:]
    else:
        if fast:
            halves_ref = refs.pop(0)
            unit_ref, mine_ref = refs[:2]
        else:
            qkv_grad_ref, proj_grad_ref = refs[:2]
        table_ref, small_ref = refs[2:4]
        refs = refs[4:]
    if not last:
        logit_out_ref, router_grad_ref, buffer_ref = refs[:3]
        refs = refs[3:]
    turned = refs.pop(0)
    if fast:
        qkv_grad_ref, proj_grad_ref = refs[:2]
        refs = refs[2:]
    if not last:
        total_ref = refs.pop(0)
    step = pl.program_id(0)
    final = pl.num_programs(0) - 1
    count, _, width = carried_ref.shape
    if fast:
        row = Row()
        if last:
            table_ref, small_ref, unit_ref, lines_ref = refs[:4]
            landing, refs = refs[4:8], refs[8:]
            above = (half_above, down_above.at[1], attn_above)
            closing = Closing(row, dp, units_ref, unit_ref, lines_ref, above, landing, refs)
        else:
            sums = RowSum(row, blocks(units_ref), refs[0], refs[1], refs[2], blocks(mine_ref), refs[3:7])
            across_x = DeepSum(dp, [mine_ref.at[0]], [refs[7]], [halves_ref], [None], [None], refs[8:10] * 4)

        def take(k):
            if closing:
                closing.take(k)
            else:
                sums.end(k)
                if k == 0:
                    across_x.over_x(k).start()

        @pl.when(step == 0)
        def _():
            if closing:
                closing.enter()
            else:
                barrier = row.greet()
                pl.semaphore_wait(barrier, 2 + across_x.greet(barrier, False))
                for k in range(2):
                    sums.start(k)

    @pl.when(step == 0)
    def _():
        qkv_grad_ref[...] = jnp.zeros(qkv_grad_ref.shape, f32)
        proj_grad_ref[...] = jnp.zeros(proj_grad_ref.shape, f32)
        table_ref[...] = jnp.zeros(table_ref.shape, f32)
        small_ref[...] = jnp.zeros(small_ref.shape, f32)
        if not last:
            total_ref[...] = jnp.zeros(total_ref.shape, f32)
            router_grad_ref[...] = jnp.zeros(router_grad_ref.shape, f32)

    pos_col = join(col_ref)[:, 0:1]
    g = join(grad_ref)
    high, low = split_two(join(logit_ref))
    gain_ref, router = gain_ref.at[0], router_ref[0]
    normed_grad = collect(pos_col, returned_ref) + nn(high, router) + nn(low, router)
    xhat, rstd = norm_parts(join(middle_ref))
    small_ref[1:2, :] += jnp.sum(normed_grad * xhat, 0, keepdims=True)
    small_ref[3:4, :] += jnp.sum(normed_grad, 0, keepdims=True)
    middle_grad = g + norm_back(normed_grad, gain_ref[1:2, :], xhat, rstd)

    def branch_part(i):
        low_part = (valid_ref[step * count + i].astype(f32) * middle_grad[image_rows(i)]).astype(bf16)
        return nn(move_ref[...], low_part)

    branch_grad = per_image(branch_part, count).astype(bf16)
    for i in range(count):
        proj_grad_ref[...] += nn(att_ref[i], branch_grad[image_rows(i)])
    att_grad = nt(proj_ref[...], branch_grad).astype(bf16)
    if fast:

        @pl.when(step == 0)
        def _():
            if closing:
                closing.early()
            else:
                for k in range(2):
                    sums.middle(k)

        pl.when(step == final)(functools.partial(take, 0))

    heads_rows = head_masks()
    halves = lane_masks()
    low_lane = iota((WPAD, LANES), 1) < WPAD
    for pair in range(PAIRS * count):
        image, side = pair // PAIRS, pair % PAIRS
        across = slice(pair * LANES, (pair + 1) * LANES)
        within = slice(side * LANES, (side + 1) * LANES)
        for group in range(HEADS // GROUP):
            features = slice(group * LANES, (group + 1) * LANES)
            grads = att_grad[features, across]
            spread = jnp.concatenate([grads * heads_rows[h] for h in range(GROUP)], 1)
            raw = nn(v_ref[image, within, features], spread)
            for h in range(GROUP):
                head = group * GROUP + h
                at = slice(head * HEAD_DIM, (head + 1) * HEAD_DIM)
                below = slice(width + head * HEAD_DIM, width + (head + 1) * HEAD_DIM)
                lowest = slice(2 * width + head * HEAD_DIM, 2 * width + (head + 1) * HEAD_DIM)
                part = raw[:, h * LANES : (h + 1) * LANES]
                probs_grad = jnp.where(low_lane, part[:WPAD], part[WPAD:])
                probs_low = probs_ref[image, side * HEADS + head]
                probs = probs_low.astype(f32)
                weighted = probs * probs_grad
                scores_grad = weighted - probs * jnp.sum(weighted, 0, keepdims=True)
                table_ref[head] += scores_grad
                scores_low = scores_grad.astype(bf16)
                both = jnp.concatenate([scores_low * halves[0], scores_low * halves[1]], 0)
                probs_both = jnp.concatenate([probs_low * halves[0], probs_low * halves[1]], 0)
                turned[at, across] = (nn(qk_ref[image, below, within], both) * head_scale).astype(bf16)
                turned[below, across] = (nt(qk_ref[image, at, within], both) * head_scale).astype(bf16)
                turned[lowest, across] = nt(att_grad[at, across], probs_both).astype(bf16)
    qkv_grad_ref[...] += nn(turned[...], join(window_ref))
    if fast:

        @pl.when(step == final)
        def _():
            columns, rows = 3 * width // mp, width // mp
            proj_turned = proj_grad_ref[...].T
            for place in range(mp):
                q = quarter_at(place, mp)
                unit_ref[place, :columns] = qkv_grad_ref[q * columns : (q + 1) * columns].astype(bf16)
                unit_ref[place, columns:] = proj_turned[q * rows : (q + 1) * rows].astype(bf16)
            take(1)
            if closing:
                closing.open()

    mixed_grad = per_image(lambda i: nt(back_ref[...], turned[:, image_rows(i)]), count).astype(bf16)
    first_grad = nn(mixed_grad, qkv_ref[...])
    if closing:

        @pl.when(step == final)
        def _():
            closing.cross()

    xhat, rstd = norm_parts(join(carried_ref))
    small_ref[0:1, :] += jnp.sum(first_grad * xhat, 0, keepdims=True)
    small_ref[2:3, :] += jnp.sum(first_grad, 0, keepdims=True)
    out = middle_grad + norm_back(first_grad, gain_ref[0:1, :], xhat, rstd)
    if last:
        top = out.astype(bf16)
        rest = out - top.astype(f32)
        mid, low = split_two(rest)
        leave = leave_ref[...]
        for i in range(count):
            at = image_rows(i)
            out_ref[i] = nn(leave, top[at]) + nn(leave, mid[at]) + nn(leave, low[at])
    else:
        store(out_ref, out)
        send_part(
            out, join(expert_out_ref), join(second_ref), router_next_ref[0], pos_col, lay_positions(row_ref), logit_out_ref,
            router_grad_ref, total_ref,
        )

    @pl.when(step == final)
    def _():
        if not last:
            buffer_ref[...] = total_ref[...].astype(bf16)
        if closing:
            heads = 2 * HEADS
            lines_ref[...] = jnp.zeros(lines_ref.shape, f32)
            lines_ref[:heads, :TABLE] = table_grad([table_ref, table_above], entry_ref[...])
            lines_ref[heads : heads + EXPERTS] = router_here[:EXPERTS]
            lines_ref[heads + EXPERTS : heads + 2 * EXPERTS] = router_above[:EXPERTS]
            lines_ref[heads + 2 * EXPERTS : heads + 2 * EXPERTS + 8] = small_ref[...]
            lines_ref[heads + 2 * EXPERTS + 8 : heads + 2 * EXPERTS + 16] = small_above[...]
            closing.finish()
            for out, landed in zip(results, landing):
                out[...] = landed[...]
        elif fast:
            across_x.halve(0)
            across_x.over_x(0).wait_send()
            for k in range(2):
                sums.finish(k)


def quarter_at(place, mp):
    return place % (mp // 2) * 2 + place // (mp // 2)


def add_up(*parts):
    total = parts[0].astype(f32)
    for part in parts[1:]:
        total = total + part.astype(f32)
    return total


def to_row(source, target, sems, k, row):
    return pltpu.make_async_remote_copy(
        src_ref=source,
        dst_ref=target,
        send_sem=sems[0].at[k],
        recv_sem=sems[1].at[k],
        device_id={"mp": row},
        device_id_type=MESH,
    )


class Row:
    def __init__(self):
        row = lax.axis_index("mp")
        self.row, self.core, self.y = row, lax.rem(row, 2), lax.div(row, 2)
        self.sibling, self.across = row + 1 - 2 * self.core, row + 2 - 4 * self.y
        self.place = self.core * 2 + self.y
        self.place_across = self.core * 2 + 1 - self.y

    def greet(self):
        barrier = pltpu.get_barrier_semaphore()
        for row in (self.sibling, self.across):
            pl.semaphore_signal(barrier, inc=1, device_id={"mp": row}, device_id_type=MESH)
        return barrier


class RowSum:
    semaphores = 4

    def __init__(self, row, units, core_in, y_out, y_in, mine, sems):
        self.row, self.units, self.mine = row, units, mine
        self.core_in, self.y_out, self.y_in = core_in, y_out, y_in
        self.sems = (sems[:2], sems[2:])

    def pair(self, k):
        theirs = self.units[k].at[pl.ds(2 * (1 - self.row.core), 2)]
        return to_row(theirs, self.core_in.at[k], self.sems[0], k, self.row.sibling)

    def cross(self, k):
        return to_row(self.y_out.at[k], self.y_in.at[k], self.sems[1], k, self.row.across)

    def start(self, k):
        self.pair(k).start()

    def middle(self, k):
        self.pair(k).wait_recv()
        other = 1 - self.row.y
        mixed = add_up(self.units[k][self.row.core * 2 + other], self.core_in[k, other])
        self.y_out[k] = mixed.astype(bf16)
        self.cross(k).start()

    def end(self, k):
        self.cross(k).wait_recv()
        self.mine[k][...] = add_up(
            self.units[k][self.row.place], self.core_in[k, self.row.y], self.y_in[k]
        ).astype(bf16)

    def finish(self, k):
        self.pair(k).wait_send()
        self.cross(k).wait_send()

    @classmethod
    def scratch(cls, count, width):
        return [
            pltpu.VMEM((count, 2, width, width), bf16),
            pltpu.VMEM((count, width, width), bf16),
            pltpu.VMEM((count, width, width), bf16),
        ] + [pltpu.SemaphoreType.DMA((count,))] * cls.semaphores


class RowGather:
    semaphores = 6

    def __init__(self, row, sources, fulls, slot, slot_across, sems):
        self.row, self.sources, self.fulls = row, sources, fulls
        self.slot, self.slot_across = slot, slot_across
        self.sems = (sems[:2], sems[2:4], sems[4:])

    def over(self, k):
        return to_row(self.sources[k], self.fulls[k].at[self.slot], self.sems[0], k, self.row.across)

    def near(self, k):
        return to_row(self.sources[k], self.fulls[k].at[self.slot], self.sems[1], k, self.row.sibling)

    def onward(self, k):
        block = self.fulls[k].at[self.slot_across]
        return to_row(block, block, self.sems[2], k, self.row.sibling)

    def start(self, k):
        self.over(k).start()
        self.near(k).start()

    def forward(self, k):
        self.over(k).wait_recv()
        self.onward(k).start()

    def arrive(self, k):
        self.near(k).wait_recv()
        self.onward(k).wait_recv()

    def sent(self, k):
        self.over(k).wait_send()
        self.near(k).wait_send()
        self.onward(k).wait_send()

    @classmethod
    def scratch(cls, count):
        return [pltpu.SemaphoreType.DMA((count,))] * cls.semaphores


class WeightGather(RowGather):
    def __init__(self, shards, fulls, sems):
        row = Row()
        super().__init__(row, shards, fulls, row.row, row.across, sems[:6])
        self.own_sem = sems[6]

    def own(self, k):
        return pltpu.make_async_copy(self.sources[k], self.fulls[k].at[self.slot], self.own_sem.at[k])

    def start(self, k):
        super().start(k)
        self.own(k).start()

    def arrive(self, k):
        super().arrive(k)
        self.own(k).wait()

    @classmethod
    def scratch(cls, count):
        return super().scratch(count) + [pltpu.SemaphoreType.DMA((count,))]


class DeepSum:
    def __init__(self, dp, total, arrived, halves, slots, result, sems):
        self.total, self.arrived, self.halves, self.slots, self.result = total, arrived, halves, slots, result
        self.x_sems, self.z_sems, self.z_back, self.x_back = (sems[2 * k : 2 * k + 2] for k in range(4))
        me = lax.axis_index("dp")
        self.x, self.z, self.deep = lax.rem(me, 2), lax.div(me, 2), dp // 2
        self.partner = me + 1 - 2 * self.x

    def greet(self, barrier, whole=True):
        pl.semaphore_signal(barrier, inc=1, device_id={"dp": self.partner}, device_id_type=MESH)
        if not whole:
            return 1
        for off in range(1, self.deep):
            peer = lax.rem(self.z + off, self.deep) * 2 + self.x
            pl.semaphore_signal(barrier, inc=1, device_id={"dp": peer}, device_id_type=MESH)
        return self.deep

    def cut(self, k):
        height = self.halves[k].shape[0]
        return height, height // self.deep

    def over_x(self, k):
        height, _ = self.cut(k)
        away = self.total[k].at[pl.ds(pl.multiple_of((1 - self.x) * height, height), height)]
        return to_peer(away, self.arrived[k], self.x_sems[0].at[k], self.x_sems[1].at[k], self.partner)

    def over_z(self, k, off):
        _, piece = self.cut(k)
        to = lax.rem(self.z + off, self.deep)
        part = self.halves[k].at[pl.ds(pl.multiple_of(to * piece, piece), piece)]
        sems = [sem.at[k, off] for sem in self.z_sems]
        return to_peer(part, self.slots[k].at[off], *sems, to * 2 + self.x)

    def own_piece(self, k):
        height, piece = self.cut(k)
        return self.result[k].at[pl.ds(pl.multiple_of(self.x * height + self.z * piece, piece), piece)]

    def own_half(self, k):
        height, _ = self.cut(k)
        return self.result[k].at[pl.ds(pl.multiple_of(self.x * height, height), height)]

    def back_z(self, k, off):
        to = lax.rem(self.z + off, self.deep)
        sems = [sem.at[k, off] for sem in self.z_back]
        return to_peer(self.own_piece(k), self.own_piece(k), *sems, to * 2 + self.x)

    def back_x(self, k):
        return to_peer(self.own_half(k), self.own_half(k), self.x_back[0].at[k], self.x_back[1].at[k], self.partner)

    def halve(self, k):
        self.over_x(k).wait_recv()
        height, _ = self.cut(k)
        keep = self.total[k][pl.ds(pl.multiple_of(self.x * height, height), height)]
        self.halves[k][...] = add_up(keep, self.arrived[k][...]).astype(self.halves[k].dtype)

    def deepen(self, k):
        for off in range(1, self.deep):
            self.over_z(k, off).start()

    def quarter(self, k):
        for off in range(1, self.deep):
            self.over_z(k, off).wait_recv()
        _, piece = self.cut(k)
        keep = self.halves[k][pl.ds(pl.multiple_of(self.z * piece, piece), piece)]
        total = add_up(keep, *[self.slots[k][off] for off in range(1, self.deep)])
        self.own_piece(k)[...] = total.astype(self.result[k].dtype)
        for off in range(1, self.deep):
            self.back_z(k, off).start()

    def widen(self, k):
        for off in range(1, self.deep):
            self.back_z(k, off).wait_recv()
        self.back_x(k).start()

    def finish(self, k, halved=True):
        if halved:
            self.over_x(k).wait_send()
        for off in range(1, self.deep):
            self.over_z(k, off).wait_send()
            self.back_z(k, off).wait_send()
        self.back_x(k).wait()

    @staticmethod
    def semaphores(dp, count):
        one, many = pltpu.SemaphoreType.DMA((count,)), pltpu.SemaphoreType.DMA((count, dp // 2))
        return [one, one, many, many, many, many, one, one]


def blocks(ref):
    return [ref.at[k] for k in range(ref.shape[0])]


class Closing:
    lines = 64

    def __init__(self, row, dp, units_ref, attn_ref, lines_ref, given, results, refs):
        self.row, self.lines_ref = row, lines_ref
        self.full, shard, small, above = results
        core_in, y_out, y_in = refs[:3]
        mine, x_in, half, z_in, self.s_core, self.s_one, self.s_y, self.s_mine, s_x, s_half, s_z = refs[7:18]
        x_above, half_above, z_above = refs[18:21]
        refs_sems, refs = refs[3:7], refs[21:]
        self.mine = mine
        self.sums = RowSum(row, blocks(units_ref) + [attn_ref], core_in, y_out, y_in, blocks(mine), refs_sems)
        self.gather = RowGather(
            row, [mine.at[k] for k in range(2)], blocks(self.full), row.place, row.place_across, refs[:6]
        )
        self.s_pair = to_row(lines_ref, self.s_core, refs[6:8], 0, row.sibling)
        self.s_cross = to_row(self.s_one, self.s_y, refs[8:10], 0, row.across)
        self.here = DeepSum(
            dp, blocks(mine) + [self.s_mine], blocks(x_in) + [s_x], blocks(half) + [s_half], blocks(z_in) + [s_z],
            blocks(shard) + [small], refs[10:18],
        )
        self.above = DeepSum(
            dp, [None, *given[1:]], [None] + blocks(x_above), [given[0]] + blocks(half_above), blocks(z_above), blocks(above),
            refs[18:26],
        )

    def enter(self):
        barrier = self.row.greet()
        pl.semaphore_wait(barrier, 2 + self.here.greet(barrier))
        for k in range(2):
            self.sums.start(k)
        self.above.deepen(0)
        for k in (1, 2):
            self.above.over_x(k).start()

    def early(self):
        for k in range(2):
            self.sums.middle(k)
        for k in (1, 2):
            self.above.halve(k)
            self.above.deepen(k)
        self.above.quarter(0)

    def take(self, k):
        self.sums.end(k)
        self.here.over_x(k).start()
        if k == 0:
            self.above.widen(0)
            for j in (1, 2):
                self.above.quarter(j)
        else:
            for j in (1, 2):
                self.above.widen(j)

    def open(self):
        self.sums.start(2)
        for k in range(2):
            self.here.halve(k)
            self.here.deepen(k)

    def cross(self):
        self.sums.middle(2)
        for k in range(2):
            self.here.quarter(k)

    def finish(self):
        here = self.here
        self.s_pair.start()
        self.sums.end(2)
        here.over_x(2).start()
        self.s_pair.wait_recv()
        self.s_one[...] = self.lines_ref[...] + self.s_core[...]
        self.s_cross.start()
        for k in range(2):
            self.gather.start(k)
            here.widen(k)
            self.full[k, self.row.place] = self.mine[k]
        here.halve(2)
        here.deepen(2)
        self.s_cross.wait_recv()
        self.s_mine[...] = self.s_one[...] + self.s_y[...]
        here.over_x(3).start()
        here.quarter(2)
        here.halve(3)
        here.deepen(3)
        here.widen(2)
        self.gather.forward(0)
        here.quarter(3)
        here.widen(3)
        self.gather.forward(1)
        self.s_pair.wait_send()
        self.s_cross.wait_send()
        for k in range(3):
            self.sums.finish(k)
            self.above.finish(k, k > 0)
        for k in range(2):
            self.gather.arrive(k)
            self.gather.sent(k)
        for k in range(4):
            here.finish(k)

    @classmethod
    def scratch(cls, dp, width):
        deep = dp // 2
        lines = cls.lines
        flat, half_flat = pltpu.VMEM((lines, width), f32), pltpu.VMEM((lines // 2, width), f32)
        half, slots = (width // 2, width), (3, deep, width // dp, width)
        return (
            RowSum.scratch(3, width)
            + [
                pltpu.VMEM((3, width, width), bf16),
                pltpu.VMEM((3, *half), bf16),
                pltpu.VMEM((3, *half), bf16),
                pltpu.VMEM(slots, bf16),
                flat, flat, flat, flat, half_flat, half_flat,
                pltpu.VMEM((deep, lines // dp, width), f32),
                pltpu.VMEM((2, *half), bf16),
                pltpu.VMEM((2, *half), bf16),
                pltpu.VMEM(slots, bf16),
            ]
            + RowGather.scratch(2)
            + [pltpu.SemaphoreType.DMA((1,))] * 4
            + DeepSum.semaphores(dp, 4)
            + DeepSum.semaphores(dp, 3)
        )


def format_kernel(columns, *refs):
    layers = len(refs[:-6]) // 3
    qkv_out, proj_out, core_up_out, core_down_out, up_out, down_out = refs[-6:]

    def form(ups, downs, shard):
        mp, rows = downs.shape[1], downs.shape[2]
        up_out[0, 0] = ups[0, 0].astype(f32)
        down_out[0, 0] = jnp.concatenate(
            [downs[0, q % 2 * (mp // 2) + q // 2].astype(f32) for q in range(mp)], 0
        ).T
        core_down_out[0] = shard[1, pl.ds(pl.multiple_of(pl.program_id(1) * rows, rows), rows)].astype(f32)

        @pl.when(pl.program_id(1) == 0)
        def _():
            qkv_out[0] = shard[2, :columns].astype(f32)
            proj_out[0] = shard[2, columns:].astype(f32)
            core_up_out[0] = shard[0].astype(f32)

    for layer in range(layers):
        pl.when(pl.program_id(0) == layer)(functools.partial(form, *refs[3 * layer : 3 * layer + 3]))


def format_call(fulls, shards, columns):
    layers = len(fulls)
    _, mp, width, _ = fulls[0].shape
    hidden, rows = mp * width, width // mp
    outs = [
        ((layers, columns, width), None),
        ((layers, width - columns, width), None),
        ((layers, width, width), None),
        ((layers, rows, hidden), pl.BlockSpec((1, rows, width), lambda i, j: (i, 0, j))),
        ((layers, 1, width, hidden), pl.BlockSpec((1, 1, width, width), lambda i, j: (i, 0, 0, j))),
        ((layers, 1, hidden, width), pl.BlockSpec((1, 1, width, width), lambda i, j: (i, 0, j, 0))),
    ]

    def by_layer(shape):
        return pl.BlockSpec((1, *shape[1:]), lambda i, j: (i, 0, 0))

    def chunk(layer, i, j):
        return jnp.where(i == layer, j, jnp.where(i < layer, 0, mp - 1))

    def place(q):
        return lax.rem(q, 2) * (mp // 2) + lax.div(q, 2)

    specs, arrays = [], []
    for layer in range(layers):
        specs += [
            pl.BlockSpec((1, 1, width, width), lambda i, j, at=layer: (0, place(chunk(at, i, j)), 0, 0)),
            pl.BlockSpec((1, mp, rows, width), lambda i, j, at=layer: (1, 0, chunk(at, i, j), 0)),
            pl.BlockSpec((3, width, width), lambda i, j: (0, 0, 0)),
        ]
        arrays += [fulls[layer], fulls[layer], shards[layer]]
    return pl.pallas_call(
        functools.partial(format_kernel, columns),
        grid=(layers, mp),
        out_shape=[jax.ShapeDtypeStruct(shape, f32) for shape, _ in outs],
        in_specs=specs,
        out_specs=[spec or by_layer(shape) for shape, spec in outs],
        compiler_params=pltpu.CompilerParams(vmem_limit_bytes=56 * MIB),
        name="format",
    )(*arrays)


def greet(dp, me, rows=()):
    barrier = pltpu.get_barrier_semaphore()
    for row in rows:
        pl.semaphore_signal(barrier, inc=1, device_id={"mp": row}, device_id_type=MESH)

    def signal(off, carry):
        pl.semaphore_signal(barrier, inc=1, device_id={"dp": lax.rem(me + off, dp)}, device_id_type=MESH)
        return carry

    lax.fori_loop(1, dp, signal, 0)
    pl.semaphore_wait(barrier, dp - 1 + len(rows))


def partner_of(me, p, dp):
    out, bit = 0, 1
    while bit < dp:
        one, two = lax.rem(lax.div(me, bit), 2), lax.rem(lax.div(p, bit), 2)
        out = out + bit * (one + two - 2 * one * two)
        bit *= 2
    return out


def to_peer(source, target, send_sem, recv_sem, peer):
    return pltpu.make_async_remote_copy(
        src_ref=source,
        dst_ref=target,
        send_sem=send_sem,
        recv_sem=recv_sem,
        device_id={"dp": peer},
        device_id_type=MESH,
    )


def gelu_parts(h):
    root = np.float32(np.sqrt(2.0 / np.pi))
    square = h * h
    t = jnp.tanh(root * h * (1.0 + 0.044715 * square))
    half = 0.5 * (1.0 + t)
    slope = half + 0.5 * h * (1.0 - t * t) * root * (1.0 + 3 * 0.044715 * square)
    return h * half, slope


def expert_forward_kernel(dp, mp, layer, gather, *refs):
    refs = list(refs)
    buffer_ref, up_any, down_any, rup_any, rdown_any = refs[:5]
    refs = refs[5:]
    if gather:
        shards = [ref.at[layer + 1] for ref in refs[:4]]
        refs = refs[4:]
    recv_ref, returned_ref, up_eff, down_eff = refs[:4]
    refs = refs[4:]
    if gather:
        fulls = refs[:4]
        refs = refs[4:]
    part, core, up_ref, down_ref, rup_ref, rdown_ref, local = refs[:7]
    refs = refs[7:]
    moving = WeightGather(shards, fulls, refs[:7]) if gather else None
    send_one, recv_one, send_two, recv_two = refs[-4:]
    split = dp // EXPERTS
    me = lax.axis_index("dp")
    loads = [
        pltpu.make_async_copy(source, target, local.at[k])
        for k, (source, target) in enumerate(
            [
                (up_any, up_ref),
                (rup_any.at[layer, 0], rup_ref),
                (down_any, down_ref),
                (rdown_any.at[layer, 0], rdown_ref),
            ]
        )
    ]
    for load in loads:
        load.start()
    greet(dp, me, (moving.row.sibling, moving.row.across) if gather else ())

    def first(off):
        peer = partner_of(me, off, dp)
        return to_peer(
            buffer_ref.at[lax.div(peer, split)], recv_ref.at[me], send_one.at[off], recv_one.at[off], peer
        )

    def second(off):
        source = partner_of(me, off, dp)
        return to_peer(part.at[source], returned_ref.at[me], send_two.at[off], recv_two.at[off], source)

    def start_first(off, carry):
        first(dp - off).start()
        return carry

    lax.fori_loop(1, dp, start_first, 0)
    if gather:
        for k in range(4):
            moving.start(k)
    recv_ref[me] = buffer_ref[lax.div(me, split)]
    hidden = up_eff.shape[1]
    columns = up_ref.shape[-1]
    loads[0].wait()
    loads[1].wait()
    if split == 1 and columns % LANES == 0:
        for m in range(mp):
            at = slice(m * columns, (m + 1) * columns)
            up_eff[:, at] = (up_ref[m].astype(f32) + rup_ref[:, at].astype(f32)).astype(bf16)
    else:
        core[...] = rup_ref[...].astype(f32)
        begin = lax.rem(me, split) * hidden
        for m in range(mp):
            put = onehot(iota((columns, hidden), 0) + m * columns == iota((columns, hidden), 1) + begin)
            core[...] += nn(up_ref[m], put)
        up_eff[...] = core[...].astype(bf16)
    begin = pl.multiple_of(lax.rem(me, split) * hidden, LANES)
    loads[2].wait()
    loads[3].wait()
    core_part = down_ref[:, :, pl.ds(begin, hidden)].reshape(down_eff.shape[1], hidden)
    down_eff[...] = (core_part.astype(f32).T + rdown_ref[...].astype(f32)).astype(bf16)

    def work(source):
        hidden_pre = nn(recv_ref[source], up_eff[...])
        hidden_low = gelu_parts(hidden_pre)[0].astype(bf16)
        return nn(hidden_low, down_eff[...]).astype(bf16)

    returned_ref[me] = work(me)

    def step(off, carry):
        source = partner_of(me, off, dp)
        first(off).wait_recv()
        part[source] = work(source)
        second(off).start()
        return carry

    lax.fori_loop(1, dp, step, 0)
    if gather:
        for k in range(4):
            moving.forward(k)

    def finish(off, carry):
        first(off).wait_send()
        second(off).wait()
        return carry

    lax.fori_loop(1, dp, finish, 0)
    if gather:
        for k in range(4):
            moving.arrive(k)
            moving.sent(k)


def expert_backward_kernel(dp, mp, fast, reduce, *refs):
    refs = list(refs)
    buffer_ref, recv_ref, up_ref, down_ref = refs[:4]
    refs = refs[4:]
    if reduce:
        given_ref, attn_ref = refs[:2]
        refs = refs[2:]
    returned_ref = refs.pop(0)
    if fast:
        units_ref = refs.pop(0)
    else:
        up_term, down_term = refs[:2]
        refs = refs[2:]
    if reduce:
        full_ref, mine_ref = refs[:2]
        refs = refs[2:]
    grads, hidden_low, slope, pre, part = refs[:5]
    refs = refs[5:]
    if fast:
        up_term, down_term = refs[:2]
        refs = refs[2:]
    row = Row() if reduce else None
    if reduce:
        core_in, y_out, y_in = refs[:3]
        sums = RowSum(row, [attn_ref], core_in, y_out, y_in, [mine_ref], refs[3:7])
        gather = RowGather(
            row, [given_ref.at[k] for k in range(2)], [full_ref.at[k] for k in range(2)], row.place, row.place_across,
            refs[7:13],
        )
        refs = refs[13:]
    send_one, recv_one, send_two, recv_two = refs
    split = dp // EXPERTS
    me = lax.axis_index("dp")
    greet(dp, me, (row.sibling, row.across) if reduce else ())

    def first(off):
        peer = partner_of(me, off, dp)
        return to_peer(buffer_ref.at[lax.div(peer, split)], grads.at[me], send_one.at[off], recv_one.at[off], peer)

    def second(off):
        source = partner_of(me, off, dp)
        return to_peer(part.at[source], returned_ref.at[me], send_two.at[off], recv_two.at[off], source)

    def start_first(off, carry):
        first(dp - off).start()
        return carry

    lax.fori_loop(1, dp, start_first, 0)
    if reduce:
        sums.start(0)
        for k in range(2):
            gather.start(k)
    grads[me] = buffer_ref[lax.div(me, split)]

    def again(source, carry):
        value, rate = gelu_parts(nn(recv_ref[source], up_ref[...]))
        hidden_low[source] = value.astype(bf16)
        slope[source] = rate
        return carry

    lax.fori_loop(0, dp, again, 0)
    if reduce:
        sums.middle(0)
        for k in range(2):
            full_ref[k, row.place] = given_ref[k]

    def work(source):
        hidden_grad = nt(grads[source], down_ref[...])
        pre_grad = (slope[source] * hidden_grad).astype(bf16)
        pre[source] = pre_grad
        return nt(pre_grad, up_ref[...]).astype(bf16)

    returned_ref[me] = work(me)

    def step(off, carry):
        source = partner_of(me, off, dp)
        first(off).wait_recv()
        part[source] = work(source)
        second(off).start()
        return carry

    lax.fori_loop(1, dp, step, 0)
    if reduce:
        for k in range(2):
            gather.forward(k)
        sums.end(0)
    up_term[...] = jnp.zeros(up_term.shape, f32)
    down_term[...] = jnp.zeros(down_term.shape, f32)

    def terms(block, carry):
        up_term[...] += tn(recv_ref[block], pre[block])
        down_term[...] += tn(grads[block], hidden_low[block])
        return carry

    lax.fori_loop(0, dp, terms, 0)
    if fast:
        width = up_term.shape[0]
        height = width // mp
        for place in range(mp):
            q = quarter_at(place, mp)
            units_ref[0, place] = up_term[:, q * width : (q + 1) * width].astype(bf16)
            for chunk in range(mp):
                block = down_term[q * height : (q + 1) * height, chunk * width : (chunk + 1) * width]
                units_ref[1, place, chunk * height : (chunk + 1) * height] = block.astype(bf16)

    def finish(off, carry):
        first(off).wait_send()
        second(off).wait()
        return carry

    lax.fori_loop(1, dp, finish, 0)
    if reduce:
        sums.finish(0)
        for k in range(2):
            gather.arrive(k)
            gather.sent(k)


def expert_call(kernel, arrays, outs, scratch, dp, collective_id, name, flops, anys=(), any_outs=()):
    sems = [pltpu.SemaphoreType.DMA((dp,))] * 4
    vmem, anywhere = pl.BlockSpec(memory_space=pltpu.VMEM), pl.BlockSpec(memory_space=pl.ANY)
    return pl.pallas_call(
        kernel,
        out_shape=[jax.ShapeDtypeStruct(shape, dtype) for shape, dtype in (*outs, *any_outs)],
        in_specs=[vmem] * len(arrays) + [anywhere] * len(anys),
        out_specs=[vmem] * len(outs) + [anywhere] * len(any_outs),
        scratch_shapes=scratch + sems,
        compiler_params=pltpu.CompilerParams(
            vmem_limit_bytes=56 * MIB, collective_id=collective_id, has_side_effects=True
        ),
        cost_estimate=pl.CostEstimate(flops=flops, bytes_accessed=20 * MIB, transcendentals=0),
        name=name,
    )(*arrays, *anys)


def by_windows(grid):
    images, kinds = grid.shape[:2]
    blocks = GRID // WINDOW
    grid = grid.reshape(images, kinds, blocks, WINDOW, blocks, WINDOW).transpose(0, 1, 2, 4, 3, 5)
    grid = grid.reshape(images, kinds, blocks * blocks, WINPOS)
    grid = jnp.pad(grid, ((0, 0), (0, 0), (0, 0), (0, WPAD - WINPOS)), constant_values=-1)
    return grid.reshape(images, kinds, IMGROWS)


def per_device(
    patches,
    qkv_weight,
    proj_weight,
    core_up,
    core_down,
    residual_up,
    residual_down,
    position_bias,
    router_weight,
    norm_gain,
    norm_bias,
    cotangent,
    image_valid,
    expert_index,
    slot_index,
    region_id,
):
    dp, mp = lax.axis_size("dp"), lax.axis_size("mp")
    images, _, width = patches.shape
    split = dp // EXPERTS
    hidden = residual_up.shape[-1]
    hidden_full = core_up.shape[-1] * mp
    row_index = lax.axis_index("mp")

    fast = split == 1 and dp == 8 and mp == 4 and hidden == mp * width
    qkv_rows, proj_rows, down_rows = (a.transpose(0, 2, 1) for a in (qkv_weight, proj_weight, core_down))
    shards = (qkv_rows, proj_rows, core_up, down_rows)
    gathered = [[None] * len(shards)] * LAYERS
    if not fast:
        gathered = [[lax.all_gather(a[l], "mp", axis=0, tiled=False) for a in shards] for l in range(LAYERS)]

    position = jnp.where(slot_index >= 0, expert_index * SLOTS + slot_index, -1)
    row_form = by_windows(jnp.stack([position.reshape(images, GRID, GRID), region_id], 1))
    col_form = row_form.transpose(0, 2, 1)
    enter = jnp.asarray(enter_table(), bf16)
    leave = jnp.asarray(enter_table().T, bf16)
    moves = [jnp.asarray(move_table(l % 2 == 1), bf16) for l in range(LAYERS)]
    backs = [jnp.asarray(move_table(l % 2 == 1).T, bf16) for l in range(LAYERS)]
    table_rows = position_bias.transpose(0, 2, 1).reshape(LAYERS * HEADS, OFFSETS)
    table_rows = jnp.pad(table_rows, ((0, 0), (0, TABLE - OFFSETS)))
    entry_row, entry_col = jnp.asarray(cell_entries()[None, :]), jnp.asarray(cell_entries()[:, None])
    routers = jnp.pad(router_weight.transpose(0, 2, 1), ((0, 0), (0, LANES - EXPERTS), (0, 0)))

    token = (images, IMGROWS, width)
    buffer_shape = (ROWS, width)
    block_rows = (dp, SLOTS, width)
    pieces = (split, ROWS, width)

    def by_piece(returned):
        return returned.reshape(EXPERTS, split, SLOTS, width).transpose(1, 0, 2, 3).reshape(pieces)

    records = []
    before = None
    for l in range(LAYERS):
        first = l == 0
        gather = fast and first
        if first:
            arrays = [("image", patches), ("whole", enter)]
        else:
            arrays = [("image", before[0]), ("image", before[1]), ("whole", before[2])]
        arrays += [
            ("smem", image_valid),
            ("image", col_form),
            ("image", row_form),
            ("any", qkv_rows) if gather else ("whole", gathered[l][0]),
            ("any", proj_rows) if gather else ("whole", gathered[l][1]),
            ("whole", table_rows) if first else (l, biases),
            ("whole", moves[l]),
            ("whole", backs[l]),
            (l, norm_gain),
            (l, norm_bias),
            (l, routers),
        ]
        if first:
            arrays.append(("whole", entry_row))
        if gather:
            arrays += [("any", core_up), ("any", down_rows)]
        outs = [("image", token, f32)]
        if first:
            outs.append(("whole", (LAYERS, HEADS, WPAD, LANES), f32))
        else:
            outs.append(("image", token, f32))
        outs += [
            ("image", token, f32),
            ("image", token, bf16),
            ("image", (images, IMGROWS, 1), f32),
            ("whole", buffer_shape, bf16),
            ("image", token, bf16),
            ("image", (images, 2 * width, IMGROWS), bf16),
            ("image", token, bf16),
            ("image", (images, PAIRS * HEADS, WPAD, LANES), bf16),
            ("image", (images, width, IMGROWS), bf16),
            ("whole", (width, width), bf16),
        ]
        scratch = [pltpu.VMEM(buffer_shape, f32)]
        gathered_shapes = [(mp, *a.shape[1:]) for a in shards]
        if gather:
            outs.append(("whole", (3 * width, width), bf16))
            outs += [("any", shape, bf16) for shape in gathered_shapes[2:]]
            scratch += [pltpu.VMEM(shape, bf16) for shape in gathered_shapes[:2]] + WeightGather.scratch(4)
        results = list(
            image_call(
                functools.partial(attention_forward_kernel, first, l % 2 == 1, mp, gather),
                images, arrays, outs, scratch, f"attend_{l}", 3 * LAYERS + 1 if gather else None,
            )
        )
        if gather:
            gathered[l] = [results[-3], None] + results[-2:]
            results = results[:-3]
        carried = results.pop(0)
        if first:
            biases = results.pop(0)
        else:
            records[-1]["expert_out"] = results.pop(0)
        middle, second_low, gate, buffer = results[:4]
        gather = fast and l < LAYERS - 1
        received, returned, up_eff, down_eff, *more = expert_call(
            functools.partial(expert_forward_kernel, dp, mp, l, gather),
            [buffer.reshape(EXPERTS, SLOTS, width)],
            [
                (block_rows, bf16),
                (block_rows, bf16),
                ((width, hidden), bf16),
                ((hidden, width), bf16),
            ],
            [
                pltpu.VMEM(block_rows, bf16),
                pltpu.VMEM((8, LANES) if fast else (width, hidden), f32),
                pltpu.VMEM(gathered_shapes[2], bf16),
                pltpu.VMEM(gathered_shapes[3], bf16),
                pltpu.VMEM((width, hidden), bf16),
                pltpu.VMEM((hidden, width), bf16),
                pltpu.SemaphoreType.DMA((4,)),
            ]
            + (WeightGather.scratch(4) if gather else []),
            dp, l, f"experts_{l}", 4 * dp * SLOTS * width * hidden,
            [gathered[l][2], gathered[l][3], residual_up, residual_down, *(shards if gather else ())],
            [(shape, bf16) for shape in gathered_shapes] if gather else (),
        )
        if gather:
            gathered[l + 1] = more
        returned = by_piece(returned)
        before = (middle, gate, returned)
        records.append(
            dict(
                carried=carried, middle=middle, second_low=second_low, gate=gate, saved=results[4:], received=received,
                up_eff=up_eff, down_eff=down_eff,
            )
        )

    top = records[-1]
    block_output, grad, logit_grad, router_part, buffer = image_call(
        turn_kernel,
        images,
        [
            ("image", before[0]),
            ("image", before[1]),
            ("whole", before[2]),
            ("image", cotangent),
            ("whole", enter),
            ("whole", leave),
            ("image", col_form),
            ("image", row_form),
            ("image", top["second_low"]),
            (LAYERS - 1, routers),
        ],
        [
            ("image", patches.shape, bf16),
            ("image", token, f32),
            ("image", (images, IMGROWS, LANES), f32),
            ("whole", (LANES, width), f32),
            ("whole", buffer_shape, bf16),
        ],
        [pltpu.VMEM(buffer_shape, f32)],
        "turn",
    )
    router_parts, tables, smalls = [None] * LAYERS, [None] * LAYERS, [None] * LAYERS
    residual_sums, shard_sums = [None] * LAYERS, [None] * LAYERS
    router_parts[LAYERS - 1] = router_part
    units, attn_units, mines = [None] * LAYERS, [None] * LAYERS, [None] * LAYERS
    for l in reversed(range(LAYERS)):
        rec = records[l]
        last = l == 0
        reduce = fast and l < LAYERS - 1
        arrays = [buffer.reshape(EXPERTS, SLOTS, width), rec["received"], rec["up_eff"], rec["down_eff"]]
        outs = [(block_rows, bf16)]
        scratch = [
            pltpu.VMEM(block_rows, bf16),
            pltpu.VMEM((dp, SLOTS, hidden), bf16),
            pltpu.VMEM((dp, SLOTS, hidden), f32),
            pltpu.VMEM((dp, SLOTS, hidden), bf16),
            pltpu.VMEM(block_rows, bf16),
        ]
        if fast:
            outs.append(((2, mp, width, width), bf16))
            scratch += [pltpu.VMEM((width, hidden), f32)] * 2
        else:
            outs += [((width, hidden), f32)] * 2
        if reduce:
            arrays += [mines[l + 1], attn_units[l + 1]]
            outs += [((2, mp, width, width), bf16), ((width, width), bf16)]
            scratch += RowSum.scratch(1, width) + RowGather.scratch(2)
        results = list(
            expert_call(
                functools.partial(expert_backward_kernel, dp, mp, fast, reduce), arrays, outs, scratch, dp, LAYERS + l,
                f"experts_back_{l}", 10 * dp * SLOTS * width * hidden,
            )
        )
        returned_grad = results.pop(0)
        if fast:
            units[l] = results.pop(0)
        else:
            residual_sums[l] = lax.psum(tuple(t.astype(bf16) for t in results[:2]), "mp")
        if reduce:
            full_above, mine_above = results
        window_in, qk, v, probs, att, proj_full = rec["saved"]
        qkv_full = gathered[l][0].reshape(3 * width, width)
        arrays = [
            ("smem", image_valid),
            ("image", grad),
            ("whole", by_piece(returned_grad)),
            ("image", logit_grad),
            ("image", rec["middle"]),
            ("image", rec["carried"]),
            (l, routers),
            ("image", col_form),
            ("whole", moves[l]),
            ("whole", backs[l]),
            (l, norm_gain),
            ("whole", proj_full),
            ("whole", qkv_full),
            ("image", window_in),
            ("image", qk),
            ("image", v),
            ("image", probs),
            ("image", att),
        ]
        outs = [("image", patches.shape if last else token, f32)]
        scratch = [pltpu.VMEM((3 * width, (2 - images % 2) * IMGROWS), bf16)]
        closes = fast and last
        table_shape, small_shape = (HEADS, WPAD, LANES), (8, width)
        if fast:
            arrays.append(("whole", units[l]))
            scratch += [pltpu.VMEM((3 * width, width), f32), pltpu.VMEM((width, width), f32)]
        if closes:
            outs += [
                ("whole", (2, mp, width, width), bf16),
                ("whole", (3, width, width), bf16),
                ("whole", (Closing.lines, width), f32),
                ("whole", (3, width, width), bf16),
            ]
        else:
            if fast:
                outs += [
                    ("whole", (width // 2, width), bf16),
                    ("whole", (mp, width, width), bf16),
                    ("whole", (2, width, width), bf16),
                ]
            else:
                outs += [("whole", (3 * width, width), f32), ("whole", (width, width), f32)]
            outs += [("whole", table_shape, f32), ("whole", small_shape, f32)]
        if last:
            arrays.append(("whole", leave))
            if fast:
                arrays += [
                    ("whole", a)
                    for a in (
                        tables[1], smalls[1], router_parts[1], router_parts[0], entry_col, halves_above, mines[1],
                        mine_above,
                    )
                ]
        else:
            below = records[l - 1]
            arrays += [
                ("image", row_form),
                ("image", below["expert_out"]),
                ("image", below["second_low"]),
                (l - 1, routers),
            ]
            outs += [
                ("image", (images, IMGROWS, LANES), f32),
                ("whole", (LANES, width), f32),
                ("whole", buffer_shape, bf16),
            ]
            scratch.append(pltpu.VMEM(buffer_shape, f32))
        if closes:
            scratch += [
                pltpu.VMEM(table_shape, f32),
                pltpu.VMEM(small_shape, f32),
                pltpu.VMEM((mp, width, width), bf16),
                pltpu.VMEM((Closing.lines, width), f32),
            ]
            scratch += [pltpu.VMEM(shape, dtype) for _, shape, dtype in outs[1:5]] + Closing.scratch(dp, width)
        elif fast:
            scratch += RowSum.scratch(2, width) + [pltpu.VMEM((width // 2, width), bf16)]
            scratch += [pltpu.SemaphoreType.DMA((1,))] * 2
        results = list(
            image_call(
                functools.partial(attention_backward_kernel, last, dp, mp, fast),
                images, arrays, outs, scratch, f"attend_back_{l}", 2 * LAYERS + 1 + l if fast else None,
            )
        )
        grad = results.pop(0)
        if closes:
            full, closed, lines, shard_above = results
            continue
        if fast:
            halves_above = results.pop(0)
            attn_units[l], mines[l] = results[:2]
        else:
            qkv_part, proj_part = results[:2]
        tables[l], smalls[l] = results[2:4]
        if not last:
            logit_grad, router_parts[l - 1], buffer = results[4:]
        if fast:
            continue
        attn = (
            lax.psum_scatter(qkv_part.astype(bf16), "mp", scatter_dimension=0, tiled=True),
            lax.psum_scatter(proj_part.T.astype(bf16), "mp", scatter_dimension=0, tiled=True),
        )
        up_sum, down_sum = residual_sums[l]
        if split > 1:
            begin = lax.axis_index("dp") % split * hidden
            empty = jnp.zeros((width, hidden_full), bf16)
            up_sum = lax.dynamic_update_slice_in_dim(empty, up_sum, begin, 1)
            down_sum = lax.dynamic_update_slice_in_dim(empty, down_sum, begin, 1)
        up_columns, down_columns = core_up.shape[-1], core_down.shape[-1]
        up_shard = lax.dynamic_slice_in_dim(up_sum, row_index * up_columns, up_columns, 1)
        down_shard = lax.dynamic_slice_in_dim(down_sum, row_index * down_columns, down_columns, 0)
        shard_sums[l] = lax.psum((attn[0], attn[1], up_shard, down_shard), "dp")

    if fast:
        *attn_grads, core_up_grad, core_down_grad, residual_up_grad, residual_down_grad = format_call(
            [full, full_above], [closed, shard_above], qkv_weight.shape[-1]
        )
        attn_grads = [a.transpose(0, 2, 1) for a in attn_grads]
        core_grads = (core_up_grad, core_down_grad.transpose(0, 2, 1))
        at = LAYERS * HEADS
        table_sum = lines[:at, :OFFSETS]
        router_sum = lines[at : at + LAYERS * EXPERTS].reshape(LAYERS, EXPERTS, width)
        at += LAYERS * EXPERTS
        small_sum = lines[at : at + LAYERS * 8].reshape(LAYERS, 8, width)[:, :4]
    else:
        entry = cell_entries()[None, :] + np.array([key_base_of(key) for key in range(WPAD)])[:, None]
        entry = jnp.asarray(np.where(np.arange(WPAD)[:, None] < WINPOS, entry, -1).reshape(-1))
        entry_turned = (entry[:, None] == jnp.arange(OFFSETS)[None, :]).astype(f32)
        table_part = jnp.dot(
            jnp.stack(tables, 0).reshape(LAYERS * HEADS, WPAD * LANES), entry_turned, precision=highest
        )
        small_part = jnp.stack(smalls, 0)[:, :4]
        router_part = jnp.stack(router_parts, 0)[:, :EXPERTS]
        table_sum, small_sum, router_sum = lax.psum((table_part, small_part, router_part), ("dp", "mp"))

        def shard(k):
            return jnp.stack([shard_sums[l][k] for l in range(LAYERS)], 0).astype(f32)

        attn_grads = (shard(0).transpose(0, 2, 1), shard(1).transpose(0, 2, 1))
        core_grads = (shard(2), shard(3).transpose(0, 2, 1))
        residual_up_grad, residual_down_grad = (
            jnp.stack([residual_sums[l][k] for l in range(LAYERS)], 0).astype(f32) for k in range(2)
        )
        residual_up_grad = residual_up_grad[:, None]
        residual_down_grad = residual_down_grad.transpose(0, 2, 1)[:, None]

    return (
        block_output,
        grad,
        attn_grads[0],
        attn_grads[1],
        core_grads[0],
        core_grads[1],
        residual_up_grad,
        residual_down_grad,
        table_sum.reshape(LAYERS, HEADS, OFFSETS).transpose(0, 2, 1),
        router_sum.transpose(0, 2, 1),
        small_sum[:, 0:2],
        small_sum[:, 2:4],
    )


def solution(mesh):
    placed = (
        P(("dp", "mp"), None, None),
        P(None, None, "mp"),
        P(None, None, "mp"),
        P(None, None, "mp"),
        P(None, None, "mp"),
        P(None, "dp", None, None),
        P(None, "dp", None, None),
        P(),
        P(),
        P(),
        P(),
        P(("dp", "mp"), None, None),
        P(("dp", "mp")),
        P(("dp", "mp"), None),
        P(("dp", "mp"), None),
        P(("dp", "mp"), None, None),
    )
    return jax.shard_map(
        per_device,
        mesh=mesh,
        in_specs=placed,
        out_specs=(
            P(("dp", "mp"), None, None),
            P(("dp", "mp"), None, None),
            P(None, None, "mp"),
            P(None, None, "mp"),
            P(None, None, "mp"),
            P(None, None, "mp"),
            P(None, "dp", None, None),
            P(None, "dp", None, None),
            P(),
            P(),
            P(),
            P(),
        ),
        check_vma=False,
    )
```

profile of v0, /device:TPU:0, one launch (start us, length us, event | category | flops | bytes accessed | tf_op | source)
XLA Modules:
  0.0 353.7 jit_solution(4789731522982771574)
XLA Ops:
  0.6 0.7 add_select_fusion
  1.4 0.8 copy.51
  2.2 0.6 pad.13.refs_7_
  2.8 0.1 stack.8
  2.9 0.9 stack.9
  3.8 0.1 reshape.62
  3.9 1.4 pad.14.refs_12_.refs_13_.router_ref.refs_6_.refs_22_
  5.3 0.3 copy.61
  5.7 0.0 copy-start
  5.7 0.8 copy.53.refs_4_.refs_5_.row_ref.refs_19_
  6.5 0.0 copy-done.1
  6.5 0.9 copy.52.refs_0_
  7.4 0.0 copy-done.2
  7.4 0.9 copy.55.cotangent_ref
  8.3 0.0 copy-done
  8.3 34.7 %attend_0.1 = (f32[4,256,384]{2,1,0:T(8,128)}, f32[2,12,64,128]{3,2,1,0:T(8,128)}, f32[4,256,384]{2,1,0:T(8,128)}, bf16[4,256,384]{2,1,0:T(8,128)(2,1)}, f32[4,2...) custom-call(bf16[4,196,384]{2,1,0:T(8,128)(2,1)} %copy.52.refs_0_, ...), custom_call_target="tpu_custom_call" | custom-call | tf_op jit(solution)/shard_map/attend_0/pallas_call | solution.py:373
  43.0 40.5 %experts_0.1 = (bf16[8,128,384]{2,1,0:T(8,128)(2,1)}, bf16[8,128,384]{2,1,0:T(8,128)(2,1)}, bf16[384,1536]{1,0:T(8,128)(2,1)}, bf16[1536,384]{1,0:T(8,128)(2,1)}...) custom-call(bf16[8,128,384]{2,1,0:T(8,128)(2,1)} %bitcast.44, ...), custom_call_target="tpu_custom_call" | custom-call | flops 2415919104 | bytes 20971520 | tf_op jit(solution)/shard_map/experts_0/pallas_call | solution.py:1325
  83.5 20.0 %attend_1.1 = (f32[4,256,384]{2,1,0:T(8,128)}, f32[4,256,384]{2,1,0:T(8,128)}, f32[4,256,384]{2,1,0:T(8,128)}, bf16[4,256,384]{2,1,0:T(8,128)(2,1)}, f32[4,256,1...) custom-call(f32[4,256,384]{2,1,0:T(8,128)} %get-tuple-element.82.ref, ...), custom_call_target="tpu_custom_call" | custom-call | tf_op jit(solution)/shard_map/attend_1/pallas_call | solution.py:373
  103.5 38.9 %experts_1.1 = (bf16[8,128,384]{2,1,0:T(8,128)(2,1)}, bf16[8,128,384]{2,1,0:T(8,128)(2,1)}, bf16[384,1536]{1,0:T(8,128)(2,1)}, bf16[1536,384]{1,0:T(8,128)(2,1)}) custom-call(bf16[8,128,384]{2,1,0:T(8,128)(2,1)} %bitcast.55, bf16[4,384,384]{2,1,0:T(8,128)(2,1)} %get-tuple-element.94.refs_1_, bf16[4,96,1536]{2,1,0:T(8,128)(2,1)} %get-tuple-element.95.refs_2_, ...), custom_call_target="tpu_custom_call" | custom-call | flops 2415919104 | bytes 20971520 | tf_op jit(solution)/shard_map/experts_1/pallas_call | solution.py:1325
  142.4 9.3 %turn.1 = (bf16[4,196,384]{2,1,0:T(8,128)(2,1)}, f32[4,256,384]{2,1,0:T(8,128)}, f32[4,256,128]{2,1,0:T(8,128)}, f32[128,384]{1,0:T(8,128)}, bf16[1024,384]{1,0:T(8,128)(2,1)}) custom-call(f32[4,256,384]{2,1,0:T(8,128)} %get-tuple-element.91.prev_ref.refs_4_, f32[4,256,1]{2,1,0:T(8,128)} %get-tuple-element.92.gate_ref, bf16[1,1024,384]{2,1,0:T(8,128)(2,1)} %bitcast.46, ...), custom_call_target="tpu_custom_call" | custom-call | tf_op jit(solution)/shard_map/turn/pallas_call | solution.py:373
  151.7 2.1 copy.58
  153.9 38.8 %experts_back_1.1 = (bf16[8,128,384]{2,1,0:T(8,128)(2,1)}, bf16[2,4,384,384]{3,2,1,0:T(8,128)(2,1)}) custom-call(bf16[8,128,384]{2,1,0:T(8,128)(2,1)} %bitcast.56, bf16[8,128,384]{2,1,0:T(8,128)(2,1)} %get-tuple-element.101.refs_1_, bf16[384,1536]{1,0:T(8,128)(2,1)} %get-tuple-element.102.refs_2_, bf16[1536,384]{1,0:T(8,128)(2,1)} %get-tuple-element.103.refs_3_), custom_call_target="tpu_custom_call" | custom-call | flops 6039797760 | bytes 20971520 | tf_op jit(solution)/shard_map/experts_back_1/pallas_call | solution.py:1325
  192.7 29.1 %attend_back_1.1 = (f32[4,256,384]{2,1,0:T(8,128)}, bf16[192,384]{1,0:T(8,128)(2,1)}, bf16[4,384,384]{2,1,0:T(8,128)(2,1)}, bf16[2,384,384]{2,1,0:T(8,128)(2,1)}...) custom-call(s32[4]{0:T(128)} %refs_0_.4, ...), custom_call_target="tpu_custom_call" | custom-call | tf_op jit(solution)/shard_map/attend_back_1/pallas_call | solution.py:373
  221.8 43.4 %experts_back_0.1 = (bf16[8,128,384]{2,1,0:T(8,128)(2,1)}, bf16[2,4,384,384]{3,2,1,0:T(8,128)(2,1)}, bf16[2,4,384,384]{3,2,1,0:T(8,128)(2,1)}, bf16[384,384]{1,0:T(8,128)(2,1)}) custom-call(bf16[8,128,384]{2,1,0:T(8,128)(2,1)} %bitcast.54, bf16[8,128,384]{2,1,0:T(8,128)(2,1)} %get-tuple-element.118.refs_1_, bf16[384,1536]{1,0:T(8,128)(2,1)} %get-tuple-element.119.refs_2_, ...), custom_call_target="tpu_custom_call" | custom-call | flops 6039797760 | bytes 20971520 | tf_op jit(solution)/shard_map/experts_back_0/pallas_call | solution.py:1325
  265.2 74.0 %attend_back_0.1 = (f32[4,196,384]{2,1,0:T(8,128)}, bf16[2,4,384,384]{3,2,1,0:T(8,128)(2,1)}, bf16[3,384,384]{2,1,0:T(8,128)(2,1)}, f32[64,384]{1,0:T(8,128)}, bf16[3,384,384]{2,1,0:T(8,128)(2,1)}) custom-call(s32[4]{0:T(128)} %refs_0_.4, f32[4,256,384]{2,1,0:T(8,128)} %get-tuple-element.116.refs_1_, bf16[1,1024,384]{2,1,0:T(8,128)(2,1)} %bitcast.42, ...), custom_call_target="tpu_custom_call" | custom-call | tf_op jit(solution)/shard_map/attend_back_0/pallas_call | solution.py:373
  339.2 0.0 copy-start.3
  339.2 2.7 copy.59
  341.9 0.0 copy-done.3
  341.9 0.6 slice_bitcast_fusion
  342.5 0.6 fusion
  343.1 0.6 copy.60
  343.7 9.8 %format.1 = (f32[2,288,384]{2,1,0:T(8,128)}, f32[2,96,384]{2,1,0:T(8,128)}, f32[2,384,384]{2,1,0:T(8,128)}, f32[2,96,1536]{2,1,0:T(8,128)}, f32[2,1,384,1536]{3,2,1,0:T(8,128)}, /*index=5*/f32[2,1,1536,384]{3,2,1,0:T(8,128)}) custom-call(bf16[2,4,384,384]{3,2,1,0:T(8,128)(2,1)} %get-tuple-element.141.refs_0_.refs_1_, ...), custom_call_target="tpu_custom_call" | custom-call | tf_op jit(solution)/shard_map/format/pallas_call | solution.py:1047
  (9 shorter events, 0.1 us)
Async XLA Ops:
  1.4 5.1 %copy-start.1 = (bf16[4,196,384]{2,0,1:T(4,128)(2,1)S(1)}, bf16[4,196,384]{2,0,1:T(4,128)(2,1)}, u32[]{:S(2)}) copy-start(bf16[4,196,384]{2,0,1:T(4,128)(2,1)} %param.24) | copy-start | bytes 1806340
  5.3 2.0 copy-start.2
  5.7 2.6 copy-start
  339.2 2.7 copy-start.3
where the time goes:
time: 361 us; the launch traced here: 354 us
  Pallas kernels  339 us (94%)
  local copies, waits for them, and re-layouts  13.5 us (4%)
    pallas_call x5, Pallas kernels, image_call(): pl.pallas_call(kernel, grid=(images // count,), out_shape=[jax.ShapeDtype...  167 us
    pallas_call x4, Pallas kernels, expert_call(): pl.pallas_call(kernel, out_shape=[jax.ShapeDtypeStruct(shape, dtype) for...  162 us
    pallas_call x1, Pallas kernels, format_call(): pl.pallas_call(functools.partial(format_kernel, columns), grid=(layers, m...  9.82 us
    unnamed x14, local copies, waits for them, and re-layouts  7.5 us

commit v1 on v0

--- a/solution.py
+++ b/solution.py
@@ -577,9 +577,13 @@
                 q = quarter_at(place, mp)
                 unit_ref[place, :columns] = qkv_grad_ref[q * columns : (q + 1) * columns].astype(bf16)
                 unit_ref[place, columns:] = proj_turned[q * rows : (q + 1) * rows].astype(bf16)
+            if closing:
+                closing.open()
             take(1)
             if closing:
-                closing.open()
+                heads = 2 * HEADS
+                lines_ref[...] = jnp.zeros(lines_ref.shape, f32)
+                lines_ref[:heads, :TABLE] = table_grad([table_ref, table_above], entry_ref[...])
 
     mixed_grad = per_image(lambda i: nt(back_ref[...], turned[:, image_rows(i)]), count).astype(bf16)
     first_grad = nn(mixed_grad, qkv_ref[...])
@@ -592,6 +596,17 @@
     xhat, rstd = norm_parts(join(carried_ref))
     small_ref[0:1, :] += jnp.sum(first_grad * xhat, 0, keepdims=True)
     small_ref[2:3, :] += jnp.sum(first_grad, 0, keepdims=True)
+    if closing:
+
+        @pl.when(step == final)
+        def _():
+            heads = 2 * HEADS
+            lines_ref[heads : heads + EXPERTS] = router_here[:EXPERTS]
+            lines_ref[heads + EXPERTS : heads + 2 * EXPERTS] = router_above[:EXPERTS]
+            lines_ref[heads + 2 * EXPERTS : heads + 2 * EXPERTS + 8] = small_ref[...]
+            lines_ref[heads + 2 * EXPERTS + 8 : heads + 2 * EXPERTS + 16] = small_above[...]
+            closing.send_lines()
+
     out = middle_grad + norm_back(first_grad, gain_ref[0:1, :], xhat, rstd)
     if last:
         top = out.astype(bf16)
@@ -613,13 +628,6 @@
         if not last:
             buffer_ref[...] = total_ref[...].astype(bf16)
         if closing:
-            heads = 2 * HEADS
-            lines_ref[...] = jnp.zeros(lines_ref.shape, f32)
-            lines_ref[:heads, :TABLE] = table_grad([table_ref, table_above], entry_ref[...])
-            lines_ref[heads : heads + EXPERTS] = router_here[:EXPERTS]
-            lines_ref[heads + EXPERTS : heads + 2 * EXPERTS] = router_above[:EXPERTS]
-            lines_ref[heads + 2 * EXPERTS : heads + 2 * EXPERTS + 8] = small_ref[...]
-            lines_ref[heads + 2 * EXPERTS + 8 : heads + 2 * EXPERTS + 16] = small_above[...]
             closing.finish()
             for out, landed in zip(results, landing):
                 out[...] = landed[...]
@@ -865,16 +873,57 @@
     return [ref.at[k] for k in range(ref.shape[0])]
 
 
+class WideSum:
+    def __init__(self, dp, total, slots, result, sems):
+        self.dp, self.total, self.slots, self.result, self.sems = dp, total, slots, result, sems
+        self.me = lax.axis_index("dp")
+
+    def piece(self, ref, at):
+        size = ref.shape[0] // self.dp
+        return ref.at[pl.ds(pl.multiple_of(at * size, size), size)]
+
+    def out(self, k, p):
+        peer = partner_of(self.me, p, self.dp)
+        sems = self.sems[0].at[k, p], self.sems[1].at[k, p]
+        return to_peer(self.piece(self.total[k], peer), self.slots[k].at[p], *sems, peer)
+
+    def back(self, k, p):
+        mine = self.piece(self.result[k], self.me)
+        sems = self.sems[2].at[k, p], self.sems[3].at[k, p]
+        return to_peer(mine, mine, *sems, partner_of(self.me, p, self.dp))
+
+    def start(self, k):
+        for p in range(self.dp - 1, 0, -1):
+            self.out(k, p).start()
+
+    def middle(self, k):
+        for p in range(1, self.dp):
+            self.out(k, p).wait_recv()
+        total = add_up(self.piece(self.total[k], self.me)[...], *[self.slots[k][p] for p in range(1, self.dp)])
+        self.piece(self.result[k], self.me)[...] = total.astype(self.result[k].dtype)
+        for p in range(self.dp - 1, 0, -1):
+            self.back(k, p).start()
+
+    def finish(self, k):
+        for p in range(1, self.dp):
+            self.out(k, p).wait_send()
+            self.back(k, p).wait()
+
+    @staticmethod
+    def semaphores(dp, count):
+        return [pltpu.SemaphoreType.DMA((count, dp))] * 4
+
+
 class Closing:
     lines = 64
 
     def __init__(self, row, dp, units_ref, attn_ref, lines_ref, given, results, refs):
-        self.row, self.lines_ref = row, lines_ref
+        self.row, self.lines_ref, self.dp = row, lines_ref, dp
         self.full, shard, small, above = results
         core_in, y_out, y_in = refs[:3]
-        mine, x_in, half, z_in, self.s_core, self.s_one, self.s_y, self.s_mine, s_x, s_half, s_z = refs[7:18]
-        x_above, half_above, z_above = refs[18:21]
-        refs_sems, refs = refs[3:7], refs[21:]
+        mine, x_in, half, z_in, self.s_core, self.s_one, self.s_y, self.s_mine, s_slots, wide_in = refs[7:17]
+        x_above, half_above, z_above = refs[17:20]
+        refs_sems, refs = refs[3:7], refs[20:]
         self.mine = mine
         self.sums = RowSum(row, blocks(units_ref) + [attn_ref], core_in, y_out, y_in, blocks(mine), refs_sems)
         self.gather = RowGather(
@@ -883,17 +932,16 @@
         self.s_pair = to_row(lines_ref, self.s_core, refs[6:8], 0, row.sibling)
         self.s_cross = to_row(self.s_one, self.s_y, refs[8:10], 0, row.across)
         self.here = DeepSum(
-            dp, blocks(mine) + [self.s_mine], blocks(x_in) + [s_x], blocks(half) + [s_half], blocks(z_in) + [s_z],
-            blocks(shard) + [small], refs[10:18],
+            dp, [mine.at[0], mine.at[1]], blocks(x_in), blocks(half), blocks(z_in), [shard.at[0], shard.at[1]], refs[10:18]
         )
         self.above = DeepSum(
             dp, [None, *given[1:]], [None] + blocks(x_above), [given[0]] + blocks(half_above), blocks(z_above), blocks(above),
             refs[18:26],
         )
+        self.wide = WideSum(dp, [mine.at[2], self.s_mine], [wide_in, s_slots], [shard.at[2], small], refs[26:30])
 
     def enter(self):
-        barrier = self.row.greet()
-        pl.semaphore_wait(barrier, 2 + self.here.greet(barrier))
+        greet(self.dp, lax.axis_index("dp"), (self.row.sibling, self.row.across))
         for k in range(2):
             self.sums.start(k)
         self.above.deepen(0)
@@ -921,74 +969,72 @@
 
     def open(self):
         self.sums.start(2)
+
+    def cross(self):
+        self.sums.middle(2)
         for k in range(2):
             self.here.halve(k)
             self.here.deepen(k)
 
-    def cross(self):
-        self.sums.middle(2)
+    def send_lines(self):
+        self.s_pair.start()
         for k in range(2):
             self.here.quarter(k)
-
-    def finish(self):
-        here = self.here
-        self.s_pair.start()
-        self.sums.end(2)
-        here.over_x(2).start()
         self.s_pair.wait_recv()
         self.s_one[...] = self.lines_ref[...] + self.s_core[...]
         self.s_cross.start()
+
+    def finish(self):
+        self.sums.end(2)
+        self.wide.start(0)
+        self.s_cross.wait_recv()
+        self.s_mine[...] = self.s_one[...] + self.s_y[...]
+        self.wide.start(1)
         for k in range(2):
             self.gather.start(k)
-            here.widen(k)
             self.full[k, self.row.place] = self.mine[k]
-        here.halve(2)
-        here.deepen(2)
-        self.s_cross.wait_recv()
-        self.s_mine[...] = self.s_one[...] + self.s_y[...]
-        here.over_x(3).start()
-        here.quarter(2)
-        here.halve(3)
-        here.deepen(3)
-        here.widen(2)
-        self.gather.forward(0)
-        here.quarter(3)
-        here.widen(3)
-        self.gather.forward(1)
+        self.wide.middle(0)
+        self.wide.middle(1)
+        for k in range(2):
+            self.here.widen(k)
+        for k in range(2):
+            self.gather.forward(k)
         self.s_pair.wait_send()
         self.s_cross.wait_send()
         for k in range(3):
             self.sums.finish(k)
             self.above.finish(k, k > 0)
         for k in range(2):
+            self.here.finish(k)
+            self.wide.finish(k)
             self.gather.arrive(k)
             self.gather.sent(k)
-        for k in range(4):
-            here.finish(k)
 
     @classmethod
     def scratch(cls, dp, width):
         deep = dp // 2
         lines = cls.lines
-        flat, half_flat = pltpu.VMEM((lines, width), f32), pltpu.VMEM((lines // 2, width), f32)
-        half, slots = (width // 2, width), (3, deep, width // dp, width)
+        flat = pltpu.VMEM((lines, width), f32)
+        half, slots = (width // 2, width), (deep, width // dp, width)
         return (
             RowSum.scratch(3, width)
             + [
                 pltpu.VMEM((3, width, width), bf16),
-                pltpu.VMEM((3, *half), bf16),
-                pltpu.VMEM((3, *half), bf16),
-                pltpu.VMEM(slots, bf16),
-                flat, flat, flat, flat, half_flat, half_flat,
-                pltpu.VMEM((deep, lines // dp, width), f32),
                 pltpu.VMEM((2, *half), bf16),
                 pltpu.VMEM((2, *half), bf16),
-                pltpu.VMEM(slots, bf16),
+                pltpu.VMEM((2, *slots), bf16),
+                flat, flat, flat, flat,
+                pltpu.VMEM((dp, lines // dp, width), f32),
+                pltpu.VMEM((dp, width // dp, width), bf16),
+                pltpu.VMEM((2, *half), bf16),
+                pltpu.VMEM((2, *half), bf16),
+                pltpu.VMEM((3, *slots), bf16),
             ]
             + RowGather.scratch(2)
             + [pltpu.SemaphoreType.DMA((1,))] * 4
-            + DeepSum.semaphores(dp, 4)
+            + DeepSum.semaphores(dp, 2)
             + DeepSum.semaphores(dp, 3)
+            + WideSum.semaphores(dp, 2)
         )
 
 

time: 361 us -> 360 us (level)
  no operation moved by 1% of the time
where the time goes in v1:
time: 360 us; the launch traced here: 353 us
  Pallas kernels  337 us (94%)
  local copies, waits for them, and re-layouts  13.5 us (4%)
    pallas_call x5, Pallas kernels, image_call(): pl.pallas_call(kernel, grid=(images // count,), out_shape=[jax.ShapeDtype...  166 us
    pallas_call x4, Pallas kernels, expert_call(): pl.pallas_call(kernel, out_shape=[jax.ShapeDtypeStruct(shape, dtype) for...  162 us
    pallas_call x1, Pallas kernels, format_call(): pl.pallas_call(functools.partial(format_kernel, columns), grid=(layers, m...  9.82 us
    unnamed x14, local copies, waits for them, and re-layouts  7.5 us

profile of v1, /device:TPU:0, one launch (start us, length us, event | category | flops | bytes accessed | tf_op | source)
XLA Modules:
  0.0 352.7 jit_solution(7893672531295024220)
XLA Ops:
  0.6 0.7 add_select_fusion
  1.4 0.8 copy.51
  2.2 0.6 pad.13.refs_7_
  2.8 0.1 stack.8
  2.9 0.9 stack.9
  3.8 0.1 reshape.62
  3.9 1.4 pad.14.refs_12_.refs_13_.router_ref.refs_6_.refs_22_
  5.3 0.3 copy.61
  5.7 0.0 copy-start
  5.7 0.8 copy.53.refs_4_.refs_5_.row_ref.refs_19_
  6.5 0.0 copy-done.1
  6.5 0.9 copy.52.refs_0_
  7.4 0.0 copy-done.2
  7.4 0.9 copy.55.cotangent_ref
  8.3 0.0 copy-done
  8.3 34.7 %attend_0.1 = (f32[4,256,384]{2,1,0:T(8,128)}, f32[2,12,64,128]{3,2,1,0:T(8,128)}, f32[4,256,384]{2,1,0:T(8,128)}, bf16[4,256,384]{2,1,0:T(8,128)(2,1)}, f32[4,2...) custom-call(bf16[4,196,384]{2,1,0:T(8,128)(2,1)} %copy.52.refs_0_, ...), custom_call_target="tpu_custom_call" | custom-call | tf_op jit(solution)/shard_map/attend_0/pallas_call | solution.py:373
  43.0 40.5 %experts_0.1 = (bf16[8,128,384]{2,1,0:T(8,128)(2,1)}, bf16[8,128,384]{2,1,0:T(8,128)(2,1)}, bf16[384,1536]{1,0:T(8,128)(2,1)}, bf16[1536,384]{1,0:T(8,128)(2,1)}...) custom-call(bf16[8,128,384]{2,1,0:T(8,128)(2,1)} %bitcast.44, ...), custom_call_target="tpu_custom_call" | custom-call | flops 2415919104 | bytes 20971520 | tf_op jit(solution)/shard_map/experts_0/pallas_call | solution.py:1371
  83.5 20.0 %attend_1.1 = (f32[4,256,384]{2,1,0:T(8,128)}, f32[4,256,384]{2,1,0:T(8,128)}, f32[4,256,384]{2,1,0:T(8,128)}, bf16[4,256,384]{2,1,0:T(8,128)(2,1)}, f32[4,256,1...) custom-call(f32[4,256,384]{2,1,0:T(8,128)} %get-tuple-element.82.ref, ...), custom_call_target="tpu_custom_call" | custom-call | tf_op jit(solution)/shard_map/attend_1/pallas_call | solution.py:373
  103.5 38.9 %experts_1.1 = (bf16[8,128,384]{2,1,0:T(8,128)(2,1)}, bf16[8,128,384]{2,1,0:T(8,128)(2,1)}, bf16[384,1536]{1,0:T(8,128)(2,1)}, bf16[1536,384]{1,0:T(8,128)(2,1)}) custom-call(bf16[8,128,384]{2,1,0:T(8,128)(2,1)} %bitcast.55, bf16[4,384,384]{2,1,0:T(8,128)(2,1)} %get-tuple-element.94.refs_1_, bf16[4,96,1536]{2,1,0:T(8,128)(2,1)} %get-tuple-element.95.refs_2_, ...), custom_call_target="tpu_custom_call" | custom-call | flops 2415919104 | bytes 20971520 | tf_op jit(solution)/shard_map/experts_1/pallas_call | solution.py:1371
  142.4 9.3 %turn.1 = (bf16[4,196,384]{2,1,0:T(8,128)(2,1)}, f32[4,256,384]{2,1,0:T(8,128)}, f32[4,256,128]{2,1,0:T(8,128)}, f32[128,384]{1,0:T(8,128)}, bf16[1024,384]{1,0:T(8,128)(2,1)}) custom-call(f32[4,256,384]{2,1,0:T(8,128)} %get-tuple-element.91.prev_ref.refs_4_, f32[4,256,1]{2,1,0:T(8,128)} %get-tuple-element.92.gate_ref, bf16[1,1024,384]{2,1,0:T(8,128)(2,1)} %bitcast.46, ...), custom_call_target="tpu_custom_call" | custom-call | tf_op jit(solution)/shard_map/turn/pallas_call | solution.py:373
  151.7 2.1 copy.58
  153.9 38.8 %experts_back_1.1 = (bf16[8,128,384]{2,1,0:T(8,128)(2,1)}, bf16[2,4,384,384]{3,2,1,0:T(8,128)(2,1)}) custom-call(bf16[8,128,384]{2,1,0:T(8,128)(2,1)} %bitcast.56, bf16[8,128,384]{2,1,0:T(8,128)(2,1)} %get-tuple-element.101.refs_1_, bf16[384,1536]{1,0:T(8,128)(2,1)} %get-tuple-element.102.refs_2_, bf16[1536,384]{1,0:T(8,128)(2,1)} %get-tuple-element.103.refs_3_), custom_call_target="tpu_custom_call" | custom-call | flops 6039797760 | bytes 20971520 | tf_op jit(solution)/shard_map/experts_back_1/pallas_call | solution.py:1371
  192.7 29.1 %attend_back_1.1 = (f32[4,256,384]{2,1,0:T(8,128)}, bf16[192,384]{1,0:T(8,128)(2,1)}, bf16[4,384,384]{2,1,0:T(8,128)(2,1)}, bf16[2,384,384]{2,1,0:T(8,128)(2,1)}...) custom-call(s32[4]{0:T(128)} %refs_0_.4, ...), custom_call_target="tpu_custom_call" | custom-call | tf_op jit(solution)/shard_map/attend_back_1/pallas_call | solution.py:373
  221.8 43.4 %experts_back_0.1 = (bf16[8,128,384]{2,1,0:T(8,128)(2,1)}, bf16[2,4,384,384]{3,2,1,0:T(8,128)(2,1)}, bf16[2,4,384,384]{3,2,1,0:T(8,128)(2,1)}, bf16[384,384]{1,0:T(8,128)(2,1)}) custom-call(bf16[8,128,384]{2,1,0:T(8,128)(2,1)} %bitcast.54, bf16[8,128,384]{2,1,0:T(8,128)(2,1)} %get-tuple-element.118.refs_1_, bf16[384,1536]{1,0:T(8,128)(2,1)} %get-tuple-element.119.refs_2_, ...), custom_call_target="tpu_custom_call" | custom-call | flops 6039797760 | bytes 20971520 | tf_op jit(solution)/shard_map/experts_back_0/pallas_call | solution.py:1371
  265.2 72.9 %attend_back_0.1 = (f32[4,196,384]{2,1,0:T(8,128)}, bf16[2,4,384,384]{3,2,1,0:T(8,128)(2,1)}, bf16[3,384,384]{2,1,0:T(8,128)(2,1)}, f32[64,384]{1,0:T(8,128)}, bf16[3,384,384]{2,1,0:T(8,128)(2,1)}) custom-call(s32[4]{0:T(128)} %refs_0_.4, f32[4,256,384]{2,1,0:T(8,128)} %get-tuple-element.116.refs_1_, bf16[1,1024,384]{2,1,0:T(8,128)(2,1)} %bitcast.42, ...), custom_call_target="tpu_custom_call" | custom-call | tf_op jit(solution)/shard_map/attend_back_0/pallas_call | solution.py:373
  338.1 0.0 copy-start.3
  338.1 2.7 copy.59
  340.8 0.0 copy-done.3
  340.8 0.6 slice_bitcast_fusion
  341.4 0.6 fusion
  342.0 0.6 copy.60
  342.7 9.8 %format.1 = (f32[2,288,384]{2,1,0:T(8,128)}, f32[2,96,384]{2,1,0:T(8,128)}, f32[2,384,384]{2,1,0:T(8,128)}, f32[2,96,1536]{2,1,0:T(8,128)}, f32[2,1,384,1536]{3,2,1,0:T(8,128)}, /*index=5*/f32[2,1,1536,384]{3,2,1,0:T(8,128)}) custom-call(bf16[2,4,384,384]{3,2,1,0:T(8,128)(2,1)} %get-tuple-element.141.refs_0_.refs_1_, ...), custom_call_target="tpu_custom_call" | custom-call | tf_op jit(solution)/shard_map/format/pallas_call | solution.py:1093
  (9 shorter events, 0.1 us)
Async XLA Ops:
  1.4 5.1 %copy-start.1 = (bf16[4,196,384]{2,0,1:T(4,128)(2,1)S(1)}, bf16[4,196,384]{2,0,1:T(4,128)(2,1)}, u32[]{:S(2)}) copy-start(bf16[4,196,384]{2,0,1:T(4,128)(2,1)} %param.24) | copy-start | bytes 1806340
  5.3 2.0 copy-start.2
  5.7 2.6 copy-start
  338.1 2.7 copy-start.3
